TPU v7x, 32 devices: a whole 2x2x4 slice. The times are simulated.
32 devices in a mesh: groups: 2 (over y), fsdp: 4 (over z), tp: 4 (over x, core).
Axes of the slice: x: 2, y: 2, z: 4, core: 2. Of those that a mesh axis runs over, the one named last changes fastest.
Arguments:
- tokens: bfloat16 [1024, 4096], P(('groups', 'fsdp')), parts along dimension 0, may hold values from -16.15 to 16.15
- query_key_value_weight: bfloat16 [4096, 8, 1280], P('fsdp', 'tp'), may hold values from -0.09375 to 0.09375
- doc_lengths: int32 [16], P('groups'), parts along dimension 0, may hold values from 1 to 256, 512 in all
Outputs:
- attention_out: bfloat16 [1024, 8, 1024], P(('groups', 'fsdp'), 'tp'), parts along dimension 0
There are 2 independent parts, one for each index of `groups`. A program takes and returns all parts, laid end to end along the dimension named above; an argument that names none is the same for every part. Nothing has to cross between parts.
Inputs may be any that keep to these rules, and one draw needn't show every extreme that they name: `doc_lengths`: the lengths sum to 512 and the longest is exactly 256.
All inputs are finite; a program needn't handle non-finite values.
Results may differ from a plain program's by a relative error of at most 0.011.
Values may be sent and summed in bfloat16 or wider, within the bound.
A program may use at most 128 MiB of HBM per device.

v0:
```python
import math

import jax
import jax.numpy as jnp
from jax import lax
from jax.sharding import PartitionSpec as P

QUERY_HEADS = 64
KEY_VALUE_HEADS = 8
HEAD_WIDTH = 128


ROPE_BASE = 500000.0
NEGATIVE = -1e30


def from_behind(array, axis, by):
    count = lax.axis_size(axis)
    pairs = [(i, i + by) for i in range(count) if 0 <= i + by < count]
    return lax.ppermute(array, axis, pairs)


def doc_offsets(doc_lengths, positions):
    ends = jnp.cumsum(doc_lengths)
    passed = (ends[None, :] <= positions[:, None]).astype(jnp.int32)
    return jnp.sum(passed * doc_lengths[None, :], axis=1)


def rotate(values, relative):
    half_width = values.shape[-1] // 2
    frequency = ROPE_BASE ** (-(jnp.arange(half_width, dtype=jnp.float32) / half_width))
    angles = relative[:, None] * frequency[None, :]
    angles = angles.reshape((angles.shape[0],) + (1,) * (values.ndim - 2) + (half_width,))
    cosine = jnp.cos(angles)
    sine_part = jnp.sin(angles)
    front_half = values[..., :half_width]
    back_half = values[..., half_width:]
    return jnp.concatenate(
        [front_half * cosine - back_half * sine_part, back_half * cosine + front_half * sine_part],
        axis=-1,
    )


def attend(queries, key_rows, value_rows, positions, doc_start, key_base):
    query_count = queries.shape[0]
    local_heads = queries.shape[1]
    query_group_count = queries.shape[2]
    head_size = queries.shape[3]
    key_count = key_rows.shape[0]
    key_block = math.gcd(128, key_count)
    blocks_total = key_count // key_block
    scaling = head_size ** (-0.5)
    first_block = jnp.clip((jnp.min(doc_start) - key_base) // key_block, 0, blocks_total)
    last_block = jnp.clip((jnp.max(positions) - key_base) // key_block + 1, 0, blocks_total)

    def block_scores(block_index):
        key_piece = lax.dynamic_slice_in_dim(key_rows, block_index * key_block, key_block, 0)
        piece_scores = (
            jnp.einsum("thgd,khd->hgtk", queries, key_piece, preferred_element_type=jnp.float32)
            * scaling
        )
        key_index = key_base + block_index * key_block + jnp.arange(key_block, dtype=jnp.int32)
        allowed = (key_index[None, :] >= doc_start[:, None]) & (
            key_index[None, :] <= positions[:, None]
        )
        return (jnp.where(allowed, piece_scores, NEGATIVE), allowed)

    def find_max(block_index, running):
        piece_scores, allowed = block_scores(block_index)
        return jnp.maximum(running, jnp.max(piece_scores, axis=-1))

    start_max = jnp.full((local_heads, query_group_count, query_count), NEGATIVE, jnp.float32)
    row_max = lax.fori_loop(first_block, last_block, find_max, start_max)

    def accumulate(block_index, carry):
        total, mixed = carry
        piece_scores, allowed = block_scores(block_index)
        unscaled = jnp.where(allowed, jnp.exp(piece_scores - row_max[..., None]), 0.0)
        value_piece = lax.dynamic_slice_in_dim(value_rows, block_index * key_block, key_block, 0)
        mixed = mixed + jnp.einsum(
            "hgtk,khd->thgd",
            unscaled.astype(jnp.bfloat16),
            value_piece,
            preferred_element_type=jnp.float32,
        )
        return (total + jnp.sum(unscaled, axis=-1), mixed)

    start_total = jnp.zeros((local_heads, query_group_count, query_count), jnp.float32)
    start_mixed = jnp.zeros((query_count, local_heads, query_group_count, head_size), jnp.float32)
    weight_sum, mixed_rows = lax.fori_loop(
        first_block, last_block, accumulate, (start_total, start_mixed)
    )
    return (mixed_rows / jnp.transpose(weight_sum, (2, 0, 1))[..., None]).astype(jnp.bfloat16)


def owner_attend(queries, window_keys, window_values, positions, doc_start, key_base):
    token_count = queries.shape[0]
    query_block = math.gcd(64, token_count)
    block_count = token_count // query_block

    def one_block(block_parts):
        return attend(
            block_parts[0], window_keys, window_values, block_parts[1], block_parts[2], key_base
        )

    blocked = (
        queries.reshape((block_count, query_block) + queries.shape[1:]),
        positions.reshape(block_count, query_block),
        doc_start.reshape(block_count, query_block),
    )
    attended = lax.map(one_block, blocked)
    return attended.reshape(queries.shape)


def on_device(tokens, query_key_value_weight, doc_lengths):
    token_count = tokens.shape[0]
    device = lax.axis_index("fsdp")
    peer_count = lax.axis_size("fsdp")
    span = min(16, peer_count // 2)
    positions = device * token_count + jnp.arange(token_count, dtype=jnp.int32)
    doc_start = doc_offsets(doc_lengths, positions)
    local_heads = query_key_value_weight.shape[1]
    query_group_count = QUERY_HEADS // KEY_VALUE_HEADS
    weight_piece = lax.all_gather(query_key_value_weight, "fsdp", axis=0, tiled=True)
    row_count = weight_piece.shape[0]
    projected_rows = jnp.dot(
        tokens, weight_piece.reshape(row_count, -1), preferred_element_type=jnp.float32
    )
    projected_rows = projected_rows.reshape(
        token_count, local_heads, query_group_count + 2, HEAD_WIDTH
    )
    relative = (positions - doc_start).astype(jnp.float32)
    queries = rotate(projected_rows[:, :, :query_group_count], relative).astype(jnp.bfloat16)
    key_rows = rotate(projected_rows[:, :, query_group_count], relative).astype(jnp.bfloat16)
    value_rows = projected_rows[:, :, query_group_count + 1].astype(jnp.bfloat16)
    key_base = (device - span) * token_count

    def step_back(carry, unused):
        moved = from_behind((carry[0], carry[1]), "fsdp", 1)
        return (moved, moved)

    unused_last, stacked = lax.scan(step_back, (key_rows, value_rows), None, length=span)
    earlier_keys = stacked[0][::-1].reshape(span * token_count, local_heads, HEAD_WIDTH)
    earlier_values = stacked[1][::-1].reshape(span * token_count, local_heads, HEAD_WIDTH)
    window_keys = jnp.concatenate([earlier_keys, key_rows], axis=0)
    window_values = jnp.concatenate([earlier_values, value_rows], axis=0)
    attended = owner_attend(queries, window_keys, window_values, positions, doc_start, key_base)
    return attended.reshape(token_count, local_heads, query_group_count * HEAD_WIDTH)


def solution(mesh):
    return jax.shard_map(
        on_device,
        mesh=mesh,
        in_specs=(P(("groups", "fsdp"), None), P("fsdp", "tp", None), P("groups")),
        out_specs=P(("groups", "fsdp"), "tp", None),
        check_vma=False,
    )
```

profile of v0, /device:TPU:29, one launch (start us, length us, event | category | flops | bytes accessed | tf_op | source)
XLA Modules:
  0.0 464.6 jit_solution(12697389747659349815)
XLA Ops:
  6.5 0.7 all-gather.2.cloned.1.call-update
  7.3 0.2 reduce-window.8
  7.5 0.1 select_reduce_fusion
  7.6 0.6 reshape.179
  8.2 0.6 add_add_fusion
  8.8 0.2 multiply_cosine_fusion
  9.0 355.5 %all-gather.2.cloned.1.call-done = bf16[4096,2,1280]{2,1,0:T(2,128)(2,1)} async-done(((bf16[1024,2,1280]{2,1,0:T(2,128)(2,1)}), bf16[4096,2,1280]{2,1,0:T(2,128)(2,1)}) %all-gather.2.cloned.1.call-update) | async-done | bytes 20971536 | tf_op jit(solution)/shard_map/all_gather | solution.py:124
  364.5 51.1 %copy.38 = bf16[4096,2,1280]{0,2,1:T(8,128)(2,1)} copy(bf16[4096,2,1280]{2,1,0:T(2,128)(2,1)} %all-gather.2.cloned.1.call-done) | data formatting | bytes 41943040 | tf_op jit(solution)/shard_map/reshape | solution.py:127
  415.7 9.9 %fusion.24 = f32[128,2,10,128]{0,3,2,1:T(8,128)S(1)} fusion(bf16[2,10,128,4096]{3,2,1,0:T(8,128)(2,1)} %bitcast.110, bf16[128,4096]{1,0:T(8,128)(2,1)S(1)} %copy-done), kind=kOutput, calls=%fused_computation.38 | convolution fusion | flops 2684354560 | bytes 23330816 | tf_op jit(solution)/shard_map/dot_general | solution.py:126
  425.6 0.1 copy.32
  425.7 0.1 copy.28
  425.8 0.2 subtract_convert_fusion
  426.0 0.1 copy.30
  426.2 0.1 copy.27
  426.3 15.0 %while.79 = (s32[]{:T(128)}, bf16[128,2,128]{2,1,0:T(2,128)(2,1)S(1)}, bf16[128,2,128]{2,1,0:T(2,128)(2,1)S(1)}, bf16[2,128,2,128]{3,2,1,0:T(2,128)(2,1)S(1)}, bf16[2,128,2,128]{3,2,1,0:T(2,128)(2,1)S(1)}, /*index=5*/s32[]{:T(128)}) while((s32[]{:T(128)}, bf16[128,2,128]{2,1,0:T(2,128)(2,1)S(1)}, bf16[128,2,128]{2,1,0:T(2,128)(2,1)S(1)}, ...), condition=%wide.region_3.4_spmd, body=%wide.region_2.3_spmd.sunk | while | flops 2 | bytes 1048741 | solution.py:142
  426.3 1.3 collective-permute-start.1
  427.6 1.3 collective-permute-start
  428.9 2.4 collective-permute-done.1
  431.3 0.1 bitcast_dynamic-update-slice_fusion.5
  431.4 1.8 collective-permute-done
  433.3 0.1 bitcast_dynamic-update-slice_fusion.4
  433.4 1.3 collective-permute-start.1
  434.7 1.3 collective-permute-start
  436.0 2.4 collective-permute-done.1
  438.4 0.1 bitcast_dynamic-update-slice_fusion.5
  438.5 2.7 collective-permute-done
  441.2 0.1 bitcast_dynamic-update-slice_fusion.4
  441.3 0.1 rev.7
  441.4 0.1 rev.6
  441.6 0.2 concatenate.19
  441.8 0.5 copy.25
  442.3 0.2 concatenate.20
  442.6 0.5 copy.26
  443.0 0.3 pad_maximum_fusion
  443.4 12.4 %while.82 = (s32[]{:T(128)}, bf16[2,64,2,8,128]{4,3,2,1,0:T(8,128)(2,1)}, s32[2,64]{1,0:T(2,128)}, s32[]{:T(128)}, s32[2,64]{1,0:T(2,128)}, /*index=5*/bf16[2,64...) while((s32[]{:T(128)}, ...), condition=%wide.region_13.14_spmd, body=%wide.region_4.13_spmd.sunk | while | flops 102285744 | bytes 8938783 | solution.py:111
  443.4 1.4 fusion.42
  446.1 1.1 while.83
  446.2 0.1 compare_and_fusion.4
  446.3 0.4 fusion.46
  446.7 0.1 compare_and_fusion.4
  446.8 0.4 fusion.46
  447.3 1.8 while.84
  447.3 0.1 compare_and_fusion.5
  447.4 0.4 fusion.50
  447.9 0.3 fusion.51
  448.2 0.1 compare_and_fusion.5
  448.3 0.4 fusion.50
  448.8 0.3 fusion.51
  449.1 0.2 fusion.43
  449.3 0.2 copy_dynamic-update-slice_fusion.2
  449.5 0.8 copy-done.2
  450.3 1.4 fusion.42
  453.1 0.5 while.83
  453.1 0.1 compare_and_fusion.4
  453.2 0.4 fusion.46
  453.7 0.0 copy-start.1
  453.7 0.9 while.84
  453.7 0.1 compare_and_fusion.5
  453.8 0.4 fusion.50
  454.3 0.3 fusion.51
  454.6 0.2 fusion.43
  454.8 0.2 copy_dynamic-update-slice_fusion.2
  455.0 0.8 copy-done.2
  455.8 2.0 reshape_reshape.3
  (47 shorter events, 0.6 us)
Async XLA Ops:
  6.5 409.1 %copy-start = (bf16[128,4096]{1,0:T(8,128)(2,1)S(1)}, bf16[128,4096]{1,0:T(8,128)(2,1)}, u32[]{:S(2)}) copy-start(bf16[128,4096]{1,0:T(8,128)(2,1)} %param.11) | copy-start | bytes 3145732
  6.5 0.8 copy-start.3
  6.5 358.0 %all-gather.2.cloned.1.call-start = ((), (), s32[]{:S(2)}) async-start(), calls=%async_computation | async-start | bytes 26214400 | tf_op jit(solution)/shard_map/all_gather | solution.py:124
  426.3 5.0 %collective-permute-start.1 = (bf16[128,2,128]{2,1,0:T(2,128)(2,1)S(1)}, bf16[128,2,128]{2,1,0:T(2,128)(2,1)S(1)}, u32[]{:S(2)}, u32[]{:S(2)}) collective-permute-start(bf16[128,2,128]{2,1,0:T(2,128)(2,1)S(1)} %get-tuple-element.704), channel_id=1, source_target_pairs={{0,4},{4,8},{8,12},{1,5},{5,9},{9,13},{2,6},{6,10},{10,14},{3,7},{... | collective-permute-start | bytes 196616 | tf_op jit(solution)/shard_map/while/body/eval_jaxpr/ppermute | solution.py:20
  427.6 5.6 %collective-permute-start = (bf16[128,2,128]{2,1,0:T(2,128)(2,1)S(1)}, bf16[128,2,128]{2,1,0:T(2,128)(2,1)S(1)}, u32[]{:S(2)}, u32[]{:S(2)}) collective-permute-start(bf16[128,2,128]{2,1,0:T(2,128)(2,1)S(1)} %get-tuple-element.703), channel_id=1, source_target_pairs={{0,4},{4,8},{8,12},{1,5},{5,9},{9,13},{2,6},{6,10},{10,14},{3,7},{... | collective-permute-start | bytes 196616 | tf_op jit(solution)/shard_map/while/body/eval_jaxpr/ppermute | solution.py:20
  433.4 5.0 %collective-permute-start.1 = (bf16[128,2,128]{2,1,0:T(2,128)(2,1)S(1)}, bf16[128,2,128]{2,1,0:T(2,128)(2,1)S(1)}, u32[]{:S(2)}, u32[]{:S(2)}) collective-permute-start(bf16[128,2,128]{2,1,0:T(2,128)(2,1)S(1)} %get-tuple-element.704), channel_id=1, source_target_pairs={{0,4},{4,8},{8,12},{1,5},{5,9},{9,13},{2,6},{6,10},{10,14},{3,7},{... | collective-permute-start | bytes 196616 | tf_op jit(solution)/shard_map/while/body/eval_jaxpr/ppermute | solution.py:20
  434.7 6.5 %collective-permute-start = (bf16[128,2,128]{2,1,0:T(2,128)(2,1)S(1)}, bf16[128,2,128]{2,1,0:T(2,128)(2,1)S(1)}, u32[]{:S(2)}, u32[]{:S(2)}) collective-permute-start(bf16[128,2,128]{2,1,0:T(2,128)(2,1)S(1)} %get-tuple-element.703), channel_id=1, source_target_pairs={{0,4},{4,8},{8,12},{1,5},{5,9},{9,13},{2,6},{6,10},{10,14},{3,7},{... | collective-permute-start | bytes 196616 | tf_op jit(solution)/shard_map/while/body/eval_jaxpr/ppermute | solution.py:20
  447.3 2.0 copy-start.1
  449.5 0.8 copy-start.2
  453.7 1.1 copy-start.1
  455.0 0.8 copy-start.2
Sparse Core Ops, SparseCore 0:
  8.9 355.5 all-gather.1
where the time goes:
time: 473 us; the launch traced here: 465 us
  waiting for transfers between devices  366 us (77%)
  local copies, waits for them, and re-layouts  58.5 us (12%)
  between operations  13.6 us (3%)
  matrix products  13.2 us (3%)
  other arithmetic  5.32 us (1%)
  starting transfers between devices  5.17 us (1%)
    all_gather x1, waiting for transfers between devices, on_device(): lax.all_gather(query_key_value_weight, 'fsdp', axis=0, tiled=True)  355 us
    reshape x1, local copies, waits for them, and re-layouts, on_device(): weight_piece.reshape(row_count, -1)  51.1 us
    dot_general x1, matrix products, on_device(): jnp.dot(tokens, weight_piece.reshape(row_count, -1), preferred_element_ty...  9.87 us
  transfers between devices with their start and end apart: 5, of which 5 were waited for; matrix products, arithmetic and copies ran while one was open for 0% of the time, Pallas kernels for 0%

commit v1 on v0

v1 whole, which is shorter than its diff:
```python
import functools

import jax
import jax.numpy as jnp
import numpy as np
from jax import lax
from jax.experimental import pallas as pl
from jax.experimental.pallas import tpu as pltpu
from jax.sharding import PartitionSpec as P

HEAD_WIDTH = 128
ROPE_BASE = 500000.0
NEGATIVE = -1e30
LEVELS = 32000.0
MESH = pl.DeviceIdType.MESH


def dot(a, b):
    return jnp.dot(a, b, preferred_element_type=jnp.float32)


def dot_t(a, b):
    return lax.dot_general(a, b, (((1,), (1,)), ((), ())), preferred_element_type=jnp.float32)


def kernel(
    n, ranks, span, lengths_ref, freq_ref, tokens_ref, weight_ref, out_ref,
    raw, weights, x_own, x_in, part_out, part_in, scale_out, scale_in, own, window,
    raw_sem, x_sem, tok_send, tok_recv, share_send, share_recv,
    part_send, part_recv, scale_send, scale_recv, kv_send, kv_recv,
):
    me = lax.axis_index("fsdp")
    rank = lax.axis_index("tp")
    tok = tokens_ref.shape[0]
    rows, heads, width = weight_ref.shape
    group = width // HEAD_WIDTH - 2
    qw = group * HEAD_WIDTH
    kvw = heads * 2 * HEAD_WIDTH
    chunks = [(0, kvw)] + [(kvw + h * qw, qw) for h in range(heads)]
    count = len(chunks)
    order = list(range(1, n))
    relayed = n == 4
    inner = (me == 1) | (me == 2)

    def peer(s):
        return lax.rem(me + s, n)

    def target(s):
        if relayed and s is order[1]:
            return jnp.where(inner, jnp.where(me == 1, 3, 0), jnp.where(me == 0, 1, 2))
        return peer(s)

    block = 128
    blocks = rows // block
    raw_copies = [
        pltpu.make_async_copy(
            weight_ref.at[pl.ds(b * block, block)], raw.at[pl.ds(b * block, block)], raw_sem.at[b]
        )
        for b in range(blocks)
    ]
    for copy in raw_copies:
        copy.start()
    own_copy = pltpu.make_async_copy(
        tokens_ref.at[:, pl.ds(pl.multiple_of(me * rows, 128), rows)], x_own, x_sem
    )
    own_copy.start()
    window[...] = jnp.zeros_like(window)

    barrier = pltpu.get_barrier_semaphore()
    for s in range(1, n):
        pl.semaphore_signal(barrier, inc=1, device_id={"fsdp": peer(s)}, device_id_type=MESH)
    for d in range(1, ranks):
        pl.semaphore_signal(
            barrier, inc=1, device_id={"tp": lax.rem(rank + d, ranks)}, device_id_type=MESH
        )
    pl.semaphore_wait(barrier, n - 1 + ranks - 1)

    sub = tok // ranks
    share = pl.ds(pl.multiple_of(rank * sub, sub), sub)
    tok_copies = {}
    for s in order:
        tok_copies[s] = pltpu.make_async_remote_copy(
            src_ref=tokens_ref.at[share, pl.ds(pl.multiple_of(peer(s) * rows, 128), rows)],
            dst_ref=x_in.at[s - 1, share],
            send_sem=tok_send.at[s - 1],
            recv_sem=tok_recv.at[s - 1],
            device_id={"fsdp": peer(s)},
            device_id_type=MESH,
        )
        tok_copies[s].start()
    share_copies = {}

    def pass_round():
        for s in order:
            tok_copies[s].wait_recv()
            for d in range(1, ranks):
                share_copies[s, d] = pltpu.make_async_remote_copy(
                    src_ref=x_in.at[s - 1, share],
                    dst_ref=x_in.at[s - 1, share],
                    send_sem=share_send.at[s - 1, d - 1],
                    recv_sem=share_recv.at[s - 1, d - 1],
                    device_id={"tp": lax.rem(rank + d, ranks)},
                    device_id_type=MESH,
                )
                share_copies[s, d].start()

    mixed = heads * block
    to_row = lax.broadcasted_iota(jnp.int32, (mixed, mixed), 0)
    from_row = lax.broadcasted_iota(jnp.int32, (mixed, mixed), 1)
    pick = (from_row == (to_row % block) * heads + to_row // block).astype(jnp.bfloat16)
    for b in range(blocks):
        if b == blocks // 2:
            pass_round()
        raw_copies[b].wait()
        at = pl.ds(b * block, block)
        piece = raw[at].reshape(mixed, width)
        if heads > 1:
            piece = dot(pick, piece).astype(jnp.bfloat16)
        for h in range(heads):
            part = piece[h * block : (h + 1) * block]
            weights[at, pl.ds(h * 2 * HEAD_WIDTH, 2 * HEAD_WIDTH)] = part[:, qw:]
            weights[at, pl.ds(kvw + h * qw, qw)] = part[:, :qw]
    for s in order:
        for d in range(1, ranks):
            share_copies[s, d].wait_recv()

    def copies(c, s):
        start, size = chunks[c]
        at = pl.ds(start, size)
        slot = s - 1
        common = dict(device_id={"fsdp": target(s)}, device_id_type=MESH)
        return (
            pltpu.make_async_remote_copy(
                src_ref=part_out.at[slot, :, at],
                dst_ref=part_in.at[slot, :, at],
                send_sem=part_send.at[c, slot],
                recv_sem=part_recv.at[c, slot],
                **common,
            ),
            pltpu.make_async_remote_copy(
                src_ref=scale_out.at[slot, :, at],
                dst_ref=scale_in.at[slot, :, at],
                send_sem=scale_send.at[c, slot],
                recv_sem=scale_recv.at[c, slot],
                **common,
            ),
        )

    def received(slot, at):
        return part_in[slot, :, at].astype(jnp.int32).astype(jnp.float32) * scale_in[slot, :, at]

    def wait_recv(c, s):
        for copy in copies(c, s):
            copy.wait_recv()

    def send(c, s, relay):
        at = pl.ds(*chunks[c])
        value = dot(x_in[n - s - 1], weights[:, at])
        if relay:
            wait_recv(c, order[1])
            value = value + received(1, at) * jnp.where(inner, 1.0, 0.0)
        largest = jnp.maximum(jnp.max(jnp.abs(value), axis=0, keepdims=True), 1e-30)
        coded = jnp.round(value * (LEVELS / largest))
        part_out[s - 1, :, at] = coded.astype(jnp.int32).astype(jnp.int16)
        scale_out[s - 1, :, at] = largest * (1.0 / LEVELS)
        for copy in copies(c, s):
            copy.start()

    def own_part():
        own_copy.wait()
        for start, size in chunks:
            at = pl.ds(start, size)
            own[:, at] = dot(x_own[...], weights[:, at])

    if relayed:
        away = jnp.where(me == 2, 1, 3)
        across = 4 - away
        for c in range(count):
            send(c, order[1], False)
            send(c, away, False)
            if c == 1:
                own_part()
            if c >= 1:
                send(c - 1, across, True)
        if count == 1:
            own_part()
        send(count - 1, across, True)
    else:
        for c in range(count):
            for s in order:
                send(c, s, False)
        own_part()

    position = me * tok + lax.broadcasted_iota(jnp.int32, (tok, HEAD_WIDTH), 0)
    lane = lax.broadcasted_iota(jnp.int32, (tok, HEAD_WIDTH), 1)
    doc_start = jnp.zeros((tok, HEAD_WIDTH), jnp.int32)
    end = jnp.int32(0)
    for d in range(lengths_ref.shape[0]):
        length = lengths_ref[d]
        end = end + length
        doc_start = doc_start + jnp.where(position >= end, length, 0)
    angle = (position - doc_start).astype(jnp.float32) * freq_ref[...]
    cosine = jnp.cos(angle)
    sine = jnp.where(lane < HEAD_WIDTH // 2, -jnp.sin(angle), jnp.sin(angle))
    biases = []
    for w in range(span + 1):
        for half in range(tok // 128):
            key = (me - span + w) * tok + half * 128 + lane
            allowed = (key >= doc_start) & (key <= position)
            biases.append(jnp.where(allowed, 0.0, NEGATIVE))
    bias = jnp.concatenate(biases, axis=1)

    def rotate(u):
        return (u * cosine + pltpu.roll(u, HEAD_WIDTH // 2, 1) * sine).astype(jnp.bfloat16)

    def arrive(c):
        for s in order:
            if not (relayed and s is order[1]):
                wait_recv(c, s)

    def total(at):
        value = own[:, at]
        for s in order:
            term = received(s - 1, at)
            if relayed and s is order[1]:
                term = term * jnp.where(inner, 0.0, 1.0)
            value = value + term
        return value

    arrive(0)
    mine = pl.ds(span * tok, tok)
    for h in range(heads):
        key_at = pl.ds(2 * h * HEAD_WIDTH, HEAD_WIDTH)
        value_at = pl.ds((2 * h + 1) * HEAD_WIDTH, HEAD_WIDTH)
        window[mine, key_at] = rotate(total(key_at))
        window[mine, value_at] = total(value_at).astype(jnp.bfloat16)
    kv_copies = []
    for j in range(1, span + 1):
        copy = pltpu.make_async_remote_copy(
            src_ref=window.at[mine],
            dst_ref=window.at[pl.ds((span - j) * tok, tok)],
            send_sem=kv_send.at[j - 1],
            recv_sem=kv_recv.at[j - 1],
            device_id={"fsdp": peer(j)},
            device_id_type=MESH,
        )
        kv_copies.append(copy)

        @pl.when(me + j < n)
        def _():
            copy.start()

    for j in range(1, span + 1):

        @pl.when(me >= j)
        def _():
            kv_copies[j - 1].wait_recv()

    scaling = HEAD_WIDTH**-0.5
    for h in range(heads):
        arrive(h + 1)
        keys = window[:, pl.ds(2 * h * HEAD_WIDTH, HEAD_WIDTH)]
        values = window[:, pl.ds((2 * h + 1) * HEAD_WIDTH, HEAD_WIDTH)]
        for g in range(group):
            query = rotate(total(pl.ds(kvw + h * qw + g * HEAD_WIDTH, HEAD_WIDTH)))
            scores = dot_t(query, keys) * scaling + bias
            unscaled = jnp.exp(scores - jnp.max(scores, axis=1, keepdims=True))
            weight_sum = jnp.sum(unscaled, axis=1, keepdims=True)
            mixed_rows = dot(unscaled.astype(jnp.bfloat16), values)
            out_ref[:, pl.ds(h * qw + g * HEAD_WIDTH, HEAD_WIDTH)] = (
                mixed_rows / weight_sum
            ).astype(jnp.bfloat16)

    for s in order:
        tok_copies[s].wait_send()
        for d in range(1, ranks):
            share_copies[s, d].wait_send()
        for c in range(count):
            for copy in copies(c, s):
                copy.wait_send()
    for j in range(1, span + 1):

        @pl.when(me + j < n)
        def _():
            kv_copies[j - 1].wait_send()


def on_device(n, ranks, tokens, weight, doc_lengths):
    tok, model = tokens.shape
    rows, heads, width = weight.shape
    span = min(16, n // 2)
    group = width // HEAD_WIDTH - 2
    half = HEAD_WIDTH // 2
    frequency = np.float32(ROPE_BASE) ** (-(np.arange(half, dtype=np.float32) / np.float32(half)))
    freq = jnp.asarray(np.concatenate([frequency, frequency])[None, :].astype(np.float32))
    bf16 = jnp.bfloat16
    out = pl.pallas_call(
        functools.partial(kernel, n, ranks, span),
        out_shape=jax.ShapeDtypeStruct((tok, heads * group * HEAD_WIDTH), bf16),
        in_specs=[
            pl.BlockSpec(memory_space=pltpu.SMEM),
            pl.BlockSpec(memory_space=pltpu.VMEM),
            pl.BlockSpec(memory_space=pl.ANY),
            pl.BlockSpec(memory_space=pl.ANY),
        ],
        out_specs=pl.BlockSpec(memory_space=pltpu.VMEM),
        scratch_shapes=[
            pltpu.VMEM((rows, heads, width), bf16),
            pltpu.VMEM((rows, heads * width), bf16),
            pltpu.VMEM((tok, rows), bf16),
            pltpu.VMEM((n - 1, tok, rows), bf16),
            pltpu.VMEM((n - 1, tok, heads * width), jnp.int16),
            pltpu.VMEM((n - 1, tok, heads * width), jnp.int16),
            pltpu.VMEM((n - 1, 1, heads * width), jnp.float32),
            pltpu.VMEM((n - 1, 1, heads * width), jnp.float32),
            pltpu.VMEM((tok, heads * width), jnp.float32),
            pltpu.VMEM(((span + 1) * tok, heads * 2 * HEAD_WIDTH), bf16),
            pltpu.SemaphoreType.DMA((rows // 128,)),
            pltpu.SemaphoreType.DMA,
            pltpu.SemaphoreType.DMA((n - 1,)),
            pltpu.SemaphoreType.DMA((n - 1,)),
            pltpu.SemaphoreType.DMA((n - 1, ranks - 1)),
            pltpu.SemaphoreType.DMA((n - 1, ranks - 1)),
            pltpu.SemaphoreType.DMA((heads + 1, n - 1)),
            pltpu.SemaphoreType.DMA((heads + 1, n - 1)),
            pltpu.SemaphoreType.DMA((heads + 1, n - 1)),
            pltpu.SemaphoreType.DMA((heads + 1, n - 1)),
            pltpu.SemaphoreType.DMA((span,)),
            pltpu.SemaphoreType.DMA((span,)),
        ],
        compiler_params=pltpu.CompilerParams(
            collective_id=0, has_side_effects=True, vmem_limit_bytes=56 * 2**20
        ),
    )(doc_lengths, freq, tokens, weight)
    return out.reshape(tok, heads, group * HEAD_WIDTH)


def solution(mesh):
    return jax.shard_map(
        functools.partial(on_device, mesh.shape["fsdp"], mesh.shape["tp"]),
        mesh=mesh,
        in_specs=(P(("groups", "fsdp"), None), P("fsdp", "tp", None), P("groups")),
        out_specs=P(("groups", "fsdp"), "tp", None),
        check_vma=False,
    )
```

time: 473 us -> 78.5 us (0.17); the launches traced: 465 us -> 78.4 us
  waiting for transfers between devices: 366 us -> 0 us
  Pallas kernels: 0 us -> 76.1 us
  local copies, waits for them, and re-layouts: 58.5 us -> 2.22 us
  between operations: 13.6 us -> 0.01 us
  matrix products: 13.2 us -> 0 us
  other arithmetic: 5.32 us -> 0 us
  starting transfers between devices: 5.17 us -> 0 us
    all_gather x1 -> x0, waiting for transfers between devices: 355 us -> none  [on_device(): lax.all_gather(query_key_value_weight, 'fsdp', axis=0, tiled=True)]
    pallas_call x0 -> x1, Pallas kernels: none -> 76.1 us  [on_device(): pl.pallas_call(functools.partial(kernel, n, ranks, span), out_shape=jax.S...]
    reshape x2 -> x1, local copies, waits for them, and re-layouts: 51.8 us -> 2.22 us  [on_device(): return out.reshape(tok, heads, group * HEAD_WIDTH)]
    dot_general x10 -> x0, matrix products: 13.2 us -> none  [the longest x1 9.87 us: on_device(): jnp.dot(tokens, weight_piece.reshape(row_count, -1), preferred_element_ty...]
    ppermute x4 -> x0, waiting for transfers between devices: 9.3 us -> none  [from_behind(): return lax.ppermute(array, axis, pairs)]
    ppermute x4 -> x0, starting transfers between devices: 5.17 us -> none  [from_behind(): return lax.ppermute(array, axis, pairs)]
  transfers between devices with their start and end apart: 5 -> 0, of which waited for: 5 -> 0; matrix products, arithmetic and copies ran while one was open for 0% -> 0% of each run, Pallas kernels for 0% -> 0%
where the time goes in v1:
time: 78.5 us; the launch traced here: 78.4 us
  Pallas kernels  76.1 us (97%)
  local copies, waits for them, and re-layouts  2.22 us (3%)
    pallas_call x1, Pallas kernels, on_device(): pl.pallas_call(functools.partial(kernel, n, ranks, span), out_shape=jax.S...  76.1 us
    reshape x1, local copies, waits for them, and re-layouts, on_device(): return out.reshape(tok, heads, group * HEAD_WIDTH)  2.22 us

profile of v1, /device:TPU:29, one launch (start us, length us, event | category | flops | bytes accessed | tf_op | source)
XLA Modules:
  0.0 78.4 jit_solution(3969231516095423051)
XLA Ops:
  0.0 76.1 %shard_map.46 = bf16[128,2048]{1,0:T(8,128)(2,1)} custom-call(s32[8]{0:T(128)} %lengths_ref.1, f32[1,128]{1,0:T(1,128)} %constant.2.clone.freq_ref, bf16[128,4096]{1,0:T(8,128)(2,1)} %tokens_ref.1, bf16[1024,2,1280]{2,1,0:T(2,128)(2,1)} %weight_ref.1), custom_call_target="tpu_custom_call" | custom-call | tf_op jit(solution)/shard_map/pallas_call | solution.py:297
  76.1 2.2 %reshape.3 = bf16[128,2,1024]{2,1,0:T(2,128)(2,1)} reshape(bf16[128,2048]{1,0:T(8,128)(2,1)} %shard_map.46) | data formatting | bytes 1048576 | tf_op jit(solution)/shard_map/reshape | solution.py:335

commit v2 on v1

--- a/solution.py
+++ b/solution.py
@@ -12,6 +12,7 @@
 ROPE_BASE = 500000.0
 NEGATIVE = -1e30
 LEVELS = 32000.0
+CUTS = 1
 MESH = pl.DeviceIdType.MESH
 
 
@@ -36,27 +37,30 @@
     group = width // HEAD_WIDTH - 2
     qw = group * HEAD_WIDTH
     kvw = heads * 2 * HEAD_WIDTH
-    chunks = [(0, kvw)] + [(kvw + h * qw, qw) for h in range(heads)]
+    cut = qw // CUTS
+    chunks = [(0, kvw)] + [(kvw + q * cut, cut) for q in range(heads * CUTS)]
     count = len(chunks)
-    order = list(range(1, n))
     relayed = n == 4
+    order = [2, 1, 3] if relayed else list(range(1, n))
     inner = (me == 1) | (me == 2)
 
     def peer(s):
         return lax.rem(me + s, n)
 
     def target(s):
-        if relayed and s is order[1]:
+        if relayed and s is order[0]:
             return jnp.where(inner, jnp.where(me == 1, 3, 0), jnp.where(me == 0, 1, 2))
         return peer(s)
 
     block = 128
     blocks = rows // block
+    parts = [(pl.ds(0, rows), pl.ds(qw, 2 * HEAD_WIDTH))]
+    parts += [(pl.ds(b * block, block), pl.ds(0, qw)) for b in range(blocks)]
     raw_copies = [
         pltpu.make_async_copy(
-            weight_ref.at[pl.ds(b * block, block)], raw.at[pl.ds(b * block, block)], raw_sem.at[b]
-        )
-        for b in range(blocks)
+            weight_ref.at[r, :, columns], raw.at[r, :, columns], raw_sem.at[i]
+        )
+        for i, (r, columns) in enumerate(parts)
     ]
     for copy in raw_copies:
         copy.start()
@@ -88,41 +92,44 @@
             device_id_type=MESH,
         )
         tok_copies[s].start()
-    share_copies = {}
+
+    def share_copy(s, d):
+        return pltpu.make_async_remote_copy(
+            src_ref=x_in.at[s - 1, share],
+            dst_ref=x_in.at[s - 1, share],
+            send_sem=share_send.at[s - 1, d - 1],
+            recv_sem=share_recv.at[s - 1, d - 1],
+            device_id={"tp": lax.rem(rank + d, ranks)},
+            device_id_type=MESH,
+        )
 
     def pass_round():
         for s in order:
             tok_copies[s].wait_recv()
             for d in range(1, ranks):
-                share_copies[s, d] = pltpu.make_async_remote_copy(
-                    src_ref=x_in.at[s - 1, share],
-                    dst_ref=x_in.at[s - 1, share],
-                    send_sem=share_send.at[s - 1, d - 1],
-                    recv_sem=share_recv.at[s - 1, d - 1],
-                    device_id={"tp": lax.rem(rank + d, ranks)},
-                    device_id_type=MESH,
-                )
-                share_copies[s, d].start()
+                share_copy(s, d).start()
 
     mixed = heads * block
     to_row = lax.broadcasted_iota(jnp.int32, (mixed, mixed), 0)
     from_row = lax.broadcasted_iota(jnp.int32, (mixed, mixed), 1)
     pick = (from_row == (to_row % block) * heads + to_row // block).astype(jnp.bfloat16)
+
+    def by_head(b, columns, start, size):
+        at = pl.ds(b * block, block)
+        piece = raw[at, :, columns].reshape(mixed, size)
+        if heads > 1:
+            piece = dot(pick, piece).astype(jnp.bfloat16)
+        for h in range(heads):
+            weights[at, pl.ds(start + h * size, size)] = piece[h * block : (h + 1) * block]
+
+    raw_copies[0].wait()
+    for b in range(blocks):
+        by_head(b, parts[0][1], 0, 2 * HEAD_WIDTH)
     for b in range(blocks):
         if b == blocks // 2:
             pass_round()
-        raw_copies[b].wait()
-        at = pl.ds(b * block, block)
-        piece = raw[at].reshape(mixed, width)
-        if heads > 1:
-            piece = dot(pick, piece).astype(jnp.bfloat16)
-        for h in range(heads):
-            part = piece[h * block : (h + 1) * block]
-            weights[at, pl.ds(h * 2 * HEAD_WIDTH, 2 * HEAD_WIDTH)] = part[:, qw:]
-            weights[at, pl.ds(kvw + h * qw, qw)] = part[:, :qw]
-    for s in order:
-        for d in range(1, ranks):
-            share_copies[s, d].wait_recv()
+        raw_copies[b + 1].wait()
+        by_head(b, parts[1][1], kvw, qw)
 
     def copies(c, s):
         start, size = chunks[c]
@@ -155,9 +162,12 @@
 
     def send(c, s, relay):
         at = pl.ds(*chunks[c])
+        if c == 0:
+            for d in range(1, ranks):
+                share_copy(n - s, d).wait_recv()
         value = dot(x_in[n - s - 1], weights[:, at])
         if relay:
-            wait_recv(c, order[1])
+            wait_recv(c, order[0])
             value = value + received(1, at) * jnp.where(inner, 1.0, 0.0)
         largest = jnp.maximum(jnp.max(jnp.abs(value), axis=0, keepdims=True), 1e-30)
         coded = jnp.round(value * (LEVELS / largest))
@@ -176,7 +186,7 @@
         away = jnp.where(me == 2, 1, 3)
         across = 4 - away
         for c in range(count):
-            send(c, order[1], False)
+            send(c, order[0], False)
             send(c, away, False)
             if c == 1:
                 own_part()
@@ -215,14 +225,14 @@
 
     def arrive(c):
         for s in order:
-            if not (relayed and s is order[1]):
+            if not (relayed and s is order[0]):
                 wait_recv(c, s)
 
     def total(at):
         value = own[:, at]
         for s in order:
             term = received(s - 1, at)
-            if relayed and s is order[1]:
+            if relayed and s is order[0]:
                 term = term * jnp.where(inner, 0.0, 1.0)
             value = value + term
         return value
@@ -258,10 +268,11 @@
 
     scaling = HEAD_WIDTH**-0.5
     for h in range(heads):
-        arrive(h + 1)
         keys = window[:, pl.ds(2 * h * HEAD_WIDTH, HEAD_WIDTH)]
         values = window[:, pl.ds((2 * h + 1) * HEAD_WIDTH, HEAD_WIDTH)]
         for g in range(group):
+            if g % (group // CUTS) == 0:
+                arrive(1 + (h * group + g) // (group // CUTS))
             query = rotate(total(pl.ds(kvw + h * qw + g * HEAD_WIDTH, HEAD_WIDTH)))
             scores = dot_t(query, keys) * scaling + bias
             unscaled = jnp.exp(scores - jnp.max(scores, axis=1, keepdims=True))
@@ -274,7 +285,7 @@
     for s in order:
         tok_copies[s].wait_send()
         for d in range(1, ranks):
-            share_copies[s, d].wait_send()
+            share_copy(s, d).wait_send()
         for c in range(count):
             for copy in copies(c, s):
                 copy.wait_send()
@@ -315,16 +326,16 @@
             pltpu.VMEM((n - 1, 1, heads * width), jnp.float32),
             pltpu.VMEM((tok, heads * width), jnp.float32),
             pltpu.VMEM(((span + 1) * tok, heads * 2 * HEAD_WIDTH), bf16),
-            pltpu.SemaphoreType.DMA((rows // 128,)),
+            pltpu.SemaphoreType.DMA((rows // 128 + 1,)),
             pltpu.SemaphoreType.DMA,
             pltpu.SemaphoreType.DMA((n - 1,)),
             pltpu.SemaphoreType.DMA((n - 1,)),
             pltpu.SemaphoreType.DMA((n - 1, ranks - 1)),
             pltpu.SemaphoreType.DMA((n - 1, ranks - 1)),
-            pltpu.SemaphoreType.DMA((heads + 1, n - 1)),
-            pltpu.SemaphoreType.DMA((heads + 1, n - 1)),
-            pltpu.SemaphoreType.DMA((heads + 1, n - 1)),
-            pltpu.SemaphoreType.DMA((heads + 1, n - 1)),
+            pltpu.SemaphoreType.DMA((heads * CUTS + 1, n - 1)),
+            pltpu.SemaphoreType.DMA((heads * CUTS + 1, n - 1)),
+            pltpu.SemaphoreType.DMA((heads * CUTS + 1, n - 1)),
+            pltpu.SemaphoreType.DMA((heads * CUTS + 1, n - 1)),
             pltpu.SemaphoreType.DMA((span,)),
             pltpu.SemaphoreType.DMA((span,)),
         ],

time: 78.5 us -> 74.5 us (0.949)
  the two profiles are of different devices: /device:TPU:29 before, /device:TPU:21 now
where the time goes in v2:
time: 74.5 us; the launch traced here: 74.4 us
  Pallas kernels  72.2 us (97%)
  local copies, waits for them, and re-layouts  2.22 us (3%)
    pallas_call x1, Pallas kernels, on_device(): pl.pallas_call(functools.partial(kernel, n, ranks, span), out_shape=jax.S...  72.2 us
    reshape x1, local copies, waits for them, and re-layouts, on_device(): return out.reshape(tok, heads, group * HEAD_WIDTH)  2.22 us

profile of v2, /device:TPU:21, one launch (start us, length us, event | category | flops | bytes accessed | tf_op | source)
XLA Modules:
  0.0 74.4 jit_solution(7634883823662562630)
XLA Ops:
  0.0 72.2 %shard_map.46 = bf16[128,2048]{1,0:T(8,128)(2,1)} custom-call(s32[8]{0:T(128)} %lengths_ref.1, f32[1,128]{1,0:T(1,128)} %constant.2.clone.freq_ref, bf16[128,4096]{1,0:T(8,128)(2,1)} %tokens_ref.1, bf16[1024,2,1280]{2,1,0:T(2,128)(2,1)} %weight_ref.1), custom_call_target="tpu_custom_call" | custom-call | tf_op jit(solution)/shard_map/pallas_call | solution.py:308
  72.2 2.2 %reshape.3 = bf16[128,2,1024]{2,1,0:T(2,128)(2,1)} reshape(bf16[128,2048]{1,0:T(8,128)(2,1)} %shard_map.46) | data formatting | bytes 1048576 | tf_op jit(solution)/shard_map/reshape | solution.py:346
